TPU v7x, 512 devices: a whole 4x4x16 slice. The times are simulated.
512 devices in a mesh: row: 16 (over y, z_hi), col: 32 (over x, z_lo, core).
Axes of the slice: x: 4, y: 4, z: 16 (z_hi: 4, z_lo: 4; z = z_hi * 4 + z_lo), core: 2. Of those that a mesh axis runs over, the one named last changes fastest.
Arguments:
- factor: float32 [8, 16, 128, 4, 32, 128], P(None, 'row', None, None, 'col'), may hold values from -0.0234375 to 0.0234375
- diag_inverse: float32 [4, 1, 32, 128, 2, 16, 128], P(None, None, 'col', None, None, 'row'), may hold values from -1 to 2
- right_side: float32 [4, 32, 128, 512], P(None, 'col'), may hold values from -6 to 6
Outputs:
- solution: float32 [8, 16, 128, 512], P(None, 'row')
All inputs are finite; a program needn't handle non-finite values.
Results may differ from a plain program's by a relative error of at most 0.0001.
Values sent between devices are 32-bit elements; how exact they have to be, the bound alone decides.
A program may use at most 64 MiB of HBM per device.

v0:
```python
import jax
import jax.numpy as jnp
from jax import lax
from jax.sharding import PartitionSpec as P


def contract_rows(matrix, vectors):
    return lax.dot_general(
        matrix,
        vectors,
        (((0,), (0,)), ((), ())),
        precision=lax.Precision.HIGHEST,
        preferred_element_type=jnp.float32,
    )


def reduce_rows(partial_value):
    return lax.psum(partial_value, "row")


def reduce_cols(products):
    return lax.psum(products, "col")


def substitute(upper_tiles, inverse, targets, panels, col_rows, own_rows):
    solved = []
    for step_index in range(panels):
        current = targets[step_index * col_rows : (step_index + 1) * col_rows]
        if step_index > 0:
            earlier = jnp.concatenate(solved, axis=0)
            partial_value = contract_rows(
                upper_tiles[
                    : step_index * own_rows, step_index * col_rows : (step_index + 1) * col_rows
                ],
                earlier,
            )
            current = current - reduce_rows(partial_value)
        solved.append(reduce_cols(contract_rows(inverse[step_index], current)))
    return jnp.concatenate(solved, axis=0)


def shards(factor, diag_inverse, right_side):
    tile_size = factor.shape[2]
    row_tiles = factor.shape[0]
    col_tiles = factor.shape[3]
    columns = right_side.shape[3]
    panels = diag_inverse.shape[0]
    upper_tiles = factor.reshape(row_tiles * tile_size, col_tiles * tile_size)
    col_rows = diag_inverse.shape[1] * tile_size
    own_rows = diag_inverse.shape[4] * tile_size
    inverse = diag_inverse.reshape(panels, col_rows, own_rows)
    targets = right_side.reshape(col_tiles * tile_size, columns)
    pieces = substitute(upper_tiles, inverse, targets, panels, col_rows, own_rows)
    return pieces.reshape(row_tiles, 1, tile_size, columns)


def solution(mesh):
    return jax.shard_map(
        shards,
        mesh=mesh,
        in_specs=(
            P(None, "row", None, None, "col", None),
            P(None, None, "col", None, None, "row", None),
            P(None, "col", None, None),
        ),
        out_specs=P(None, "row", None, None),
        check_vma=False,
    )
```

profile of v0, /device:TPU:1, one launch (start us, length us, event | category | flops | bytes accessed | tf_op | source)
XLA Modules:
  0.0 1783.2 jit_solution(13683338339830794248)
XLA Ops:
  6.5 2.7 slice_reduce_fusion
  9.3 2.4 fusion.14
  11.7 0.0 all-reduce.8.cloned.1.call-update
  11.7 0.0 all-reduce.10.cloned.1.call-start
  11.7 1.8 copy.33
  13.5 289.8 %all-reduce.8.cloned.1.call-done = f32[256,512]{1,0:T(8,128)} async-done(((f32[256,512]{1,0:T(8,128)}), f32[256,512]{1,0:T(8,128)}) %all-reduce.8.cloned.1.call-update) | async-done | bytes 524304 | tf_op jit(solution)/shard_map/psum | solution.py:22
  303.3 2.3 convolution_bitcast_fusion.3
  305.6 0.0 all-reduce.12.cloned.1.call-start
  305.7 194.1 %all-reduce.10.cloned.1.call-done = f32[128,512]{1,0:T(8,128)} async-done(((f32[128,512]{1,0:T(8,128)}), f32[128,512]{1,0:T(8,128)}) %all-reduce.10.cloned.1.call-update) | async-done | bytes 262160 | tf_op jit(solution)/shard_map/psum | solution.py:18
  499.8 2.4 convolution_bitcast_fusion.2
  502.3 0.0 all-reduce.14.cloned.1.call-start
  502.3 291.3 %all-reduce.12.cloned.1.call-done = f32[256,512]{1,0:T(8,128)} async-done(((f32[256,512]{1,0:T(8,128)}), f32[256,512]{1,0:T(8,128)}) %all-reduce.12.cloned.1.call-update) | async-done | bytes 524304 | tf_op jit(solution)/shard_map/psum | solution.py:22
  793.6 2.6 convolution_bitcast_fusion.4
  796.3 0.0 all-reduce.16.cloned.1.call-start
  796.3 193.7 %all-reduce.14.cloned.1.call-done = f32[128,512]{1,0:T(8,128)} async-done(((f32[128,512]{1,0:T(8,128)}), f32[128,512]{1,0:T(8,128)}) %all-reduce.14.cloned.1.call-update) | async-done | bytes 262160 | tf_op jit(solution)/shard_map/psum | solution.py:18
  990.0 2.4 convolution_bitcast_fusion.1
  992.5 0.0 all-reduce.18.cloned.1.call-start
  992.6 291.1 %all-reduce.16.cloned.1.call-done = f32[256,512]{1,0:T(8,128)} async-done(((f32[256,512]{1,0:T(8,128)}), f32[256,512]{1,0:T(8,128)}) %all-reduce.16.cloned.1.call-update) | async-done | bytes 524304 | tf_op jit(solution)/shard_map/psum | solution.py:22
  1283.7 2.9 fusion.6
  1286.6 0.0 all-reduce.20.cloned.1.call-start
  1286.6 193.4 %all-reduce.18.cloned.1.call-done = f32[128,512]{1,0:T(8,128)} async-done(((f32[128,512]{1,0:T(8,128)}), f32[128,512]{1,0:T(8,128)}) %all-reduce.18.cloned.1.call-update) | async-done | bytes 262160 | tf_op jit(solution)/shard_map/psum | solution.py:18
  1480.1 2.4 convolution_bitcast_fusion
  1482.5 291.3 %all-reduce.20.cloned.1.call-done = f32[256,512]{1,0:T(8,128)} async-done(((f32[256,512]{1,0:T(8,128)}), f32[256,512]{1,0:T(8,128)}) %all-reduce.20.cloned.1.call-update) | async-done | bytes 524304 | tf_op jit(solution)/shard_map/psum | solution.py:22
  1773.9 2.5 pad_maximum_fusion
  (13 shorter events, 0.1 us)
Async XLA Ops:
  6.5 296.8 %all-reduce.8.cloned.1.call-start = ((), (), s32[]{:S(2)}) async-start(), calls=%async_computation | async-start | bytes 1048576 | tf_op jit(solution)/shard_map/psum | solution.py:22
  11.7 488.1 %all-reduce.10.cloned.1.call-start = ((), (), s32[]{:S(2)}) async-start(), calls=%async_computation.1 | async-start | bytes 524288 | tf_op jit(solution)/shard_map/psum | solution.py:18
  303.3 490.3 %copy-start = (f32[256,512]{1,0:T(8,128)S(1)}, f32[256,512]{1,0:T(8,128)}, u32[]{:S(2)}) copy-start(f32[256,512]{1,0:T(8,128)} %all-reduce.8.cloned.1.call-done) | copy-start | bytes 1572868
  305.6 488.0 %all-reduce.12.cloned.1.call-start = ((), (), s32[]{:S(2)}) async-start(), calls=%async_computation.2 | async-start | bytes 1048576 | tf_op jit(solution)/shard_map/psum | solution.py:22
  502.3 487.8 %all-reduce.14.cloned.1.call-start = ((), (), s32[]{:S(2)}) async-start(), calls=%async_computation.3 | async-start | bytes 524288 | tf_op jit(solution)/shard_map/psum | solution.py:18
  793.6 490.1 %copy-start.1 = (f32[256,512]{1,0:T(8,128)S(1)}, f32[256,512]{1,0:T(8,128)}, u32[]{:S(2)}) copy-start(f32[256,512]{1,0:T(8,128)} %all-reduce.12.cloned.1.call-done) | copy-start | bytes 1572868
  796.3 487.4 %all-reduce.16.cloned.1.call-start = ((), (), s32[]{:S(2)}) async-start(), calls=%async_computation.4 | async-start | bytes 1048576 | tf_op jit(solution)/shard_map/psum | solution.py:22
  992.5 487.6 %all-reduce.18.cloned.1.call-start = ((), (), s32[]{:S(2)}) async-start(), calls=%async_computation.5 | async-start | bytes 524288 | tf_op jit(solution)/shard_map/psum | solution.py:18
  1286.6 487.3 %copy-start.2 = (f32[256,512]{1,0:T(8,128)S(1)}, f32[256,512]{1,0:T(8,128)}, u32[]{:S(2)}) copy-start(f32[256,512]{1,0:T(8,128)} %all-reduce.16.cloned.1.call-done) | copy-start | bytes 1572868
  1286.6 487.3 %all-reduce.20.cloned.1.call-start = ((), (), s32[]{:S(2)}) async-start(), calls=%async_computation.6 | async-start | bytes 1048576 | tf_op jit(solution)/shard_map/psum | solution.py:22
Sparse Core Ops, SparseCore 0:
  11.8 291.4 all-reduce.7
  306.4 193.2 all-reduce.9
  502.7 290.8 all-reduce.11
  796.6 193.3 all-reduce.13
  992.8 290.8 all-reduce.15
  1286.7 193.3 all-reduce.17
  1483.0 290.8 all-reduce.19
where the time goes:
time: 1780 us
  waiting for transfers between devices  1740 us (98%)
    psum x4, waiting for transfers between devices, reduce_cols(): return lax.psum(products, 'col')  1160 us
    psum x3, waiting for transfers between devices, reduce_rows(): return lax.psum(partial_value, 'row')  581 us
  transfers between devices with their start and end apart: 7, of which 7 were waited for; matrix products, arithmetic and copies ran while one was open for 0% of the time, Pallas kernels for 0%

commit v1 on v0

v1 whole, which is shorter than its diff:
```python
import functools

import jax
import jax.numpy as jnp
from jax import lax
from jax.experimental import pallas as pl
from jax.experimental.pallas import tpu as pltpu
from jax.sharding import PartitionSpec as P

F32 = jnp.float32
BF16 = jnp.bfloat16
MESH = pl.DeviceIdType.MESH
NC = 2
KS = 64
KC = KS // NC
YC = KC // 4
PAIRS = ((0, 1), (0, 2), (1, 2), (0, 3), (1, 3), (2, 3))
BLOCK = {pair: index for index, pair in enumerate(PAIRS)}


def split(value):
    high = value.astype(BF16)
    return high, (value - high.astype(F32)).astype(BF16)


def dot3(high, low, right_high, right_low):
    rows = high.shape[0]
    both = jnp.dot(
        jnp.concatenate([high, low], axis=0), right_high, preferred_element_type=F32
    )
    cross = jnp.dot(high, right_low, preferred_element_type=F32)
    return both[:rows] + (both[rows:] + cross)


def kernel(
    fac, dinv, rhs, out,
    facv, dinvv, bv, bT, bS, bR,
    Uall, Dall, Uh, Ul, Dh, Dl,
    P0, Rc, Rx, Z, CT, Ry, H, CY, X, OT,
    lsem, ssem, rsem,
):
    row = lax.axis_index("row")
    col = lax.axis_index("col")
    y, zh = row // 4, lax.rem(row, 4)
    x, zl, co = col // 8, lax.rem(col // 2, 4), lax.rem(col, 2)

    def dev(y_, zh_, x_, zl_, co_):
        return (y_ * 4 + zh_, (x_ * 4 + zl_) * 2 + co_)

    ring = lambda at, k: lax.rem(at + k, 4)
    core_peer = dev(y, zh, x, zl, 1 - co)
    x_peer = {k: dev(y, zh, ring(x, k), zl, co) for k in (1, 2, 3)}
    xc_peer = {k: dev(y, zh, ring(x, k), zl, 1 - co) for k in (1, 2, 3)}
    y_peer = {k: dev(ring(y, k), zh, x, zl, co) for k in (1, 2, 3)}
    zh_peer = {k: dev(y, ring(zh, k), x, zl, co) for k in (1, 2, 3)}
    zl_peer = {k: dev(y, zh, x, ring(zl, k), co) for k in (1, 2, 3)}
    order = (2, 1, 3)

    started = []

    def send(src, dst, peer):
        index = len(started)
        copy = pltpu.make_async_remote_copy(
            src_ref=src, dst_ref=dst, send_sem=ssem.at[index], recv_sem=rsem.at[index],
            device_id=peer, device_id_type=MESH,
        )
        copy.start()
        started.append(copy)
        return copy

    def arrive(copies):
        for copy in copies:
            copy.wait_recv()

    loads = [
        pltpu.make_async_copy(dinv, dinvv, lsem.at[0]),
        pltpu.make_async_copy(rhs, bv, lsem.at[1]),
        pltpu.make_async_copy(fac.at[pl.ds(0, 3072)], facv, lsem.at[2]),
    ]
    for copy in loads:
        copy.start()
    barrier = pltpu.get_barrier_semaphore()
    greeted = [core_peer]
    for group in (x_peer, xc_peer, y_peer, zh_peer, zl_peer):
        greeted += [group[k] for k in order]
    for peer in greeted:
        pl.semaphore_signal(barrier, inc=1, device_id=peer, device_id_type=MESH)

    loads[0].wait()
    loads[1].wait()
    d0 = jnp.concatenate(
        [dinvv[pl.ds(a, 128, stride=2), :] for a in range(2)], axis=1
    )
    d0h, d0l = split(d0)
    b0h, b0l = split(bv[0].T)
    for half in range(2):
        for quarter in range(4):
            at = 256 * half + 64 * quarter
            value = dot3(b0h[at : at + 64], b0l[at : at + 64], d0h, d0l)
            for ch in range(NC):
                P0[half, ch, quarter] = value[ch * KC : (ch + 1) * KC]

    loads[2].wait()
    for (q, p), block in BLOCK.items():
        Uall[block, 0, 0] = facv[pl.ds(1024 * q + p, 256, stride=4), :]
    for p in range(1, 4):
        for a in range(2):
            Dall[p - 1, 0, 0, :, a * 128 : (a + 1) * 128] = dinvv[
                pl.ds(256 * p + a, 128, stride=2), :
            ]

    pl.semaphore_wait(barrier, len(greeted))

    core_copies = [
        send(P0.at[1 - co, ch], Rc.at[ch], core_peer) for ch in range(NC)
    ]

    for p in range(1, 4):
        bT[p - 1] = bv[p].T
    for dco in range(2):
        for dx in range(4):
            to_co = co if dco == 0 else 1 - co
            base = 256 * to_co + 64 * ring(x, dx) + YC * y
            for p in range(3):
                for ch in range(NC):
                    at = pl.multiple_of(base + KC * ch, 8)
                    piece = bT[p, pl.ds(at, YC), :]
                    if dco == 0 and dx == 0:
                        bR[0, p, ch] = piece
                    else:
                        bS[dco * 4 + dx, p, ch] = piece

    def spread(buffer, block):
        return [
            send(buffer.at[block, 0, 0], buffer.at[block, 0, k], x_peer[k]) for k in order
        ]

    def forward(buffer, block, copies):
        arrive(copies)
        return [send(buffer.at[block, 0], buffer.at[block, 1], core_peer)]

    def ready_u(block, copies):
        arrive(copies)

        def body(slot, carry):
            high, low = split(Uall[block, slot // 4, lax.rem(slot, 4)])
            lanes = pl.ds(pl.multiple_of(slot * 128, 128), 128)
            Uh[block, :, lanes] = high
            Ul[block, :, lanes] = low
            return carry

        lax.fori_loop(0, 8, body, 0)

    def ready_d(block, copies):
        arrive(copies)

        def body(slot, carry):
            high, low = split(Dall[block, slot // 4, lax.rem(slot, 4)])
            rows = pl.ds(pl.multiple_of(slot * 128, 128), 128)
            Dh[block, rows, :] = high
            Dl[block, rows, :] = low
            return carry

        lax.fori_loop(0, 8, body, 0)

    def share(buffer, me, peers):
        return [send(buffer.at[me], buffer.at[me], peers[k]) for k in order]

    def total(buffer):
        return (buffer[0] + buffer[1]) + (buffer[2] + buffer[3])

    x_copies = []
    for ch in range(NC):
        arrive(core_copies[ch : ch + 1])
        P0[co, ch] = P0[co, ch] + Rc[ch]
        x_copies.append(
            [send(P0.at[co, ch, ring(x, k)], Rx.at[ch, k - 1], x_peer[k]) for k in order]
        )
    b_copies = []
    for dco in range(2):
        for dx in range(4):
            if dco or dx:
                peer = (x_peer[dx] if dco == 0 else core_peer if dx == 0 else xc_peer[dx])
                b_copies.append(send(bS.at[dco * 4 + dx], bR.at[dco * 4 + dx], peer))
    u01 = spread(Uall, 0)
    z_copies = []
    for ch in range(NC):
        arrive(x_copies[ch])
        Z[0, ch, zl] = (P0[co, ch, x] + Rx[ch, 0]) + (Rx[ch, 1] + Rx[ch, 2])
        z_copies.append(share(Z.at[0, ch], zl, zl_peer))
    d1 = spread(Dall, 0)
    ready_u(0, forward(Uall, 0, u01))

    def add_update(p, q, first, count):
        block = BLOCK[(q, p)]
        high, low = split(X[q, pl.ds(first, count), :])
        for n in range(4):
            lanes = slice(256 * n, 256 * (n + 1))
            value = dot3(high, low, Uh[block, :, lanes], Ul[block, :, lanes])
            if q > 0:
                value = value + CT[p - 1, pl.ds(first, count), lanes]
            CT[p - 1, pl.ds(first, count), lanes] = value

    out_first = {}
    out_second = {}
    stores = []

    def output_first(p):
        OT[p, co, x] = X[p]
        out_first[p] = [
            send(OT.at[p, co, x], OT.at[p, co, x], x_peer[k]) for k in order
        ]

    def output_second(p):
        arrive(out_first[p])
        out_second[p] = [send(OT.at[p, co], OT.at[p, co], core_peer)]

    def output_third(p):
        arrive(out_second[p])
        copy = pltpu.make_async_copy(OT.at[p], out.at[p], lsem.at[3 + p])
        copy.start()
        stores.append(copy)

    pending = {}
    for p in range(1, 4):
        y_copies = []
        for ch in range(NC):
            arrive(z_copies[ch])
            X[p - 1, ch * KC : (ch + 1) * KC] = total(Z.at[p - 1, ch])
            add_update(p, p - 1, ch * KC, KC)
            y_copies.append([
                send(
                    CT.at[p - 1, pl.ds(pl.multiple_of(KC * ch + YC * ring(y, k), 8), YC)],
                    Ry.at[p - 1, ch, k - 1], y_peer[k],
                )
                for k in order
            ])
        output_first(p - 1)
        if p == 1:
            u02 = spread(Uall, 1)
            d1 = forward(Dall, 0, d1)
        if p == 2:
            u13 = spread(Uall, 4)
            u03 = forward(Uall, 3, u03)

        h_copies = []
        for ch in range(NC):
            arrive(y_copies[ch])
            own = CT[p - 1, pl.ds(pl.multiple_of(KC * ch + YC * y, 8), YC), :]
            H[p - 1, ch, zh] = (own + Ry[p - 1, ch, 0]) + (Ry[p - 1, ch, 1] + Ry[p - 1, ch, 2])
            h_copies.append(share(H.at[p - 1, ch], zh, zh_peer))
        if p == 1:
            arrive(b_copies)
            u12 = spread(Uall, 2)
            ready_d(0, d1)
            ready_u(1, forward(Uall, 1, u02))
            add_update(2, 0, 0, KS)
            d2 = spread(Dall, 1)
        if p == 2:
            u23 = spread(Uall, 5)
            ready_d(1, d2)
            ready_u(3, u03)
            add_update(3, 0, 0, KS)
            ready_u(4, forward(Uall, 4, u13))
            add_update(3, 1, 0, KS)
            d3 = spread(Dall, 2)
        if p == 3:
            ready_d(2, d3)
        output_second(p - 1)

        a_copies = []
        for ch in range(NC):
            arrive(h_copies[ch])
            right = jnp.concatenate([bR[slot, p - 1, ch] for slot in range(8)], axis=1)
            CY[p - 1, ch, y] = right - total(H.at[p - 1, ch])
            a_copies.append(share(CY.at[p - 1, ch], y, y_peer))
        if p == 1:
            u12 = forward(Uall, 2, u12)
        if p == 2:
            u23 = forward(Uall, 5, u23)

        z_copies = []
        for ch in range(NC):
            arrive(a_copies[ch])
            high, low = split(CY[p - 1, ch].reshape(KC, 1024))
            Z[p, ch, zl] = dot3(high, low, Dh[p - 1], Dl[p - 1])
            z_copies.append(share(Z.at[p, ch], zl, zl_peer))
        if p == 1:
            u03 = spread(Uall, 3)
            ready_u(2, u12)
            d2 = forward(Dall, 1, d2)
        if p == 2:
            ready_u(5, u23)
            d3 = forward(Dall, 2, d3)
        output_third(p - 1)

    for ch in range(NC):
        arrive(z_copies[ch])
        X[3, ch * KC : (ch + 1) * KC] = total(Z.at[3, ch])
    output_first(3)
    output_second(3)
    output_third(3)
    for copy in started:
        copy.wait_send()
    for copy in stores:
        copy.wait()


def count_sends():
    return NC + 3 * NC + 7 + 9 * 4 + 4 * 3 * NC + 9 * 3 * NC + 4 * 4


def shards(factor, diag_inverse, right_side):
    sends = count_sends()
    solved = pl.pallas_call(
        kernel,
        out_shape=jax.ShapeDtypeStruct((4, 2, 4, 64, 256), F32),
        in_specs=[pl.BlockSpec(memory_space=pl.ANY)] * 3,
        out_specs=pl.BlockSpec(memory_space=pl.ANY),
        scratch_shapes=[
            pltpu.VMEM((3072, 128), F32),
            pltpu.VMEM((1024, 128), F32),
            pltpu.VMEM((4, 128, 512), F32),
            pltpu.VMEM((3, 512, 128), F32),
            pltpu.VMEM((8, 3, NC, YC, 128), F32),
            pltpu.VMEM((8, 3, NC, YC, 128), F32),
            pltpu.VMEM((6, 2, 4, 256, 128), F32),
            pltpu.VMEM((3, 2, 4, 128, 256), F32),
            pltpu.VMEM((6, 256, 1024), BF16),
            pltpu.VMEM((6, 256, 1024), BF16),
            pltpu.VMEM((3, 1024, 256), BF16),
            pltpu.VMEM((3, 1024, 256), BF16),
            pltpu.VMEM((2, NC, 4, KC, 256), F32),
            pltpu.VMEM((NC, 4, KC, 256), F32),
            pltpu.VMEM((NC, 3, KC, 256), F32),
            pltpu.VMEM((4, NC, 4, KC, 256), F32),
            pltpu.VMEM((3, KS, 1024), F32),
            pltpu.VMEM((3, NC, 3, YC, 1024), F32),
            pltpu.VMEM((3, NC, 4, YC, 1024), F32),
            pltpu.VMEM((3, NC, 4, YC, 1024), F32),
            pltpu.VMEM((4, KS, 256), F32),
            pltpu.VMEM((4, 2, 4, 64, 256), F32),
            pltpu.SemaphoreType.DMA((7,)),
            pltpu.SemaphoreType.DMA((sends,)),
            pltpu.SemaphoreType.DMA((sends,)),
        ],
        compiler_params=pltpu.CompilerParams(
            collective_id=0, has_side_effects=True, vmem_limit_bytes=56 * 1024 * 1024
        ),
        name="substitution",
    )(
        factor.reshape(4096, 128),
        diag_inverse.reshape(1024, 128),
        right_side.reshape(4, 128, 512),
    )
    pieces = solved.reshape(4, 512, 2, 128).transpose(0, 2, 3, 1)
    return pieces.reshape(8, 1, 128, 512)


def solution(mesh):
    return jax.shard_map(
        shards,
        mesh=mesh,
        in_specs=(
            P(None, "row", None, None, "col", None),
            P(None, None, "col", None, None, "row", None),
            P(None, "col", None, None),
        ),
        out_specs=P(None, "row", None, None),
        check_vma=False,
    )
```

time: 1780 us -> 128 us (0.07)
  waiting for transfers between devices: 1740 us -> 0 us
  Pallas kernels: 0 us -> 124 us
    psum x7 -> x0, waiting for transfers between devices: 1740 us -> none  [the longest x4 1160 us: reduce_cols(): return lax.psum(products, 'col')]
    pallas_call x0 -> x1, Pallas kernels: none -> 124 us  [shards(): pl.pallas_call(kernel, out_shape=jax.ShapeDtypeStruct((4, 2, 4, 64, 256),...]
  transfers between devices with their start and end apart: 7 -> 0, of which waited for: 7 -> 0; matrix products, arithmetic and copies ran while one was open for 0% -> 0% of each run, Pallas kernels for 0% -> 0%
where the time goes in v1:
time: 128 us
  Pallas kernels  124 us (97%)
  local copies, waits for them, and re-layouts  4.62 us (4%)
    pallas_call x1, Pallas kernels, shards(): pl.pallas_call(kernel, out_shape=jax.ShapeDtypeStruct((4, 2, 4, 64, 256),...  124 us

profile of v1, /device:TPU:1, one launch (start us, length us, event | category | flops | bytes accessed | tf_op | source)
XLA Modules:
  0.0 128.3 jit_solution(6320483101314794428)
XLA Ops:
  0.0 123.6 %substitution.1 = f32[4,2,4,64,256]{4,3,2,1,0:T(8,128)} custom-call(f32[4096,128]{1,0:T(8,128)} %bitcast.8, f32[1024,128]{1,0:T(8,128)} %bitcast.10, f32[4,128,512]{2,1,0:T(8,128)} %bitcast.9), custom_call_target="tpu_custom_call" | custom-call | tf_op jit(solution)/shard_map/substitution/pallas_call | solution.py:315
  123.6 2.3 %reshape.18 = f32[4,512,2,128]{3,2,1,0:T(2,128)S(1)} reshape(f32[4,2,4,64,256]{4,3,2,1,0:T(8,128)} %substitution.1) | data formatting | bytes 4194304 | tf_op jit(solution)/shard_map/reshape | solution.py:356
  125.9 2.3 %copy.4 = f32[4,2,128,512]{3,2,1,0:T(8,128)} copy(f32[4,2,128,512]{2,1,3,0:T(2,128)S(1)} %bitcast.7) | data formatting | bytes 4194304 | tf_op jit(solution)/shard_map/transpose | solution.py:356

commit v2 on v1

--- a/solution.py
+++ b/solution.py
@@ -37,7 +37,7 @@
     facv, dinvv, bv, bT, bS, bR,
     Uall, Dall, Uh, Ul, Dh, Dl,
     P0, Rc, Rx, Z, CT, Ry, H, CY, X, OT,
-    lsem, ssem, rsem,
+    lsem, ssem, rsem, beyond,
 ):
     row = lax.axis_index("row")
     col = lax.axis_index("col")
@@ -68,6 +68,14 @@
         started.append(copy)
         return copy
 
+    marks = []
+
+    def drain():
+        marks.append(len(started))
+        if len(marks) > 3:
+            for copy in started[0 if len(marks) == 4 else marks[-5] : marks[-4]]:
+                copy.wait_send()
+
     def arrive(copies):
         for copy in copies:
             copy.wait_recv()
@@ -80,9 +88,10 @@
     for copy in loads:
         copy.start()
     barrier = pltpu.get_barrier_semaphore()
-    greeted = [core_peer]
-    for group in (x_peer, xc_peer, y_peer, zh_peer, zl_peer):
+    greeted = [zh_peer[1], zh_peer[3]]
+    for group in (zl_peer, x_peer, xc_peer, y_peer):
         greeted += [group[k] for k in order]
+    greeted.append(core_peer)
     for peer in greeted:
         pl.semaphore_signal(barrier, inc=1, device_id=peer, device_id_type=MESH)
 
@@ -110,10 +119,84 @@
             ]
 
     pl.semaphore_wait(barrier, len(greeted))
-
-    core_copies = [
-        send(P0.at[1 - co, ch], Rc.at[ch], core_peer) for ch in range(NC)
-    ]
+    for k in (1, 3):
+        pl.semaphore_signal(beyond, inc=1, device_id=zh_peer[k], device_id_type=MESH)
+
+    near, far = (1, 3), (2,)
+    spreads = {}
+
+    def spread(buffer, block, steps):
+        spreads.setdefault((buffer is Dall, block), []).extend(
+            send(buffer.at[block, 0, 0], buffer.at[block, 0, k], x_peer[k]) for k in steps
+        )
+
+    def forward(buffer, block):
+        arrive(spreads[(buffer is Dall, block)])
+        return [send(buffer.at[block, 0], buffer.at[block, 1], core_peer)]
+
+    def pass_on(block, k, index):
+        arrive(spreads[(False, block)][index : index + 1])
+        return send(Uall.at[block, 0, k], Uall.at[block, 1, k], core_peer)
+
+    def ready_u(block, copies):
+        arrive(copies)
+
+        def body(slot, carry):
+            high, low = split(Uall[block, slot // 4, lax.rem(slot, 4)])
+            lanes = pl.ds(pl.multiple_of(slot * 128, 128), 128)
+            Uh[block, :, lanes] = high
+            Ul[block, :, lanes] = low
+            return carry
+
+        lax.fori_loop(0, 8, body, 0)
+
+    def ready_d(block, copies):
+        arrive(copies)
+
+        def body(slot, carry):
+            high, low = split(Dall[block, slot // 4, lax.rem(slot, 4)])
+            rows = pl.ds(pl.multiple_of(slot * 128, 128), 128)
+            Dh[block, rows, :] = high
+            Dl[block, rows, :] = low
+            return carry
+
+        lax.fori_loop(0, 8, body, 0)
+
+    def share(buffer, me, peers):
+        return [send(buffer.at[me], buffer.at[me], peers[k]) for k in order]
+
+    def total(buffer):
+        return (buffer[0] + buffer[1]) + (buffer[2] + buffer[3])
+
+    core_copies, x_copies, z_copies = {}, {}, {}
+
+    def over_core(ch):
+        core_copies[ch] = [send(P0.at[1 - co, ch], Rc.at[ch], core_peer)]
+
+    def over_x(ch):
+        arrive(core_copies[ch])
+        P0[co, ch] = P0[co, ch] + Rc[ch]
+        x_copies[ch] = [
+            send(P0.at[co, ch, ring(x, k)], Rx.at[ch, k - 1], x_peer[k]) for k in order
+        ]
+
+    def over_z(ch):
+        arrive(x_copies[ch])
+        Z[0, ch, zl] = (P0[co, ch, x] + Rx[ch, 0]) + (Rx[ch, 1] + Rx[ch, 2])
+        z_copies[ch] = share(Z.at[0, ch], zl, zl_peer)
+
+    spread(Uall, 0, near)
+    for ch in range(NC):
+        over_core(ch)
+    spread(Uall, 0, far)
+    u01 = [send(Uall.at[0, 0, 0], Uall.at[0, 1, 0], core_peer)]
+    for ch in range(NC):
+        over_x(ch)
+    u01 += [pass_on(0, k, index) for index, k in enumerate(near)]
+    for ch in range(NC):
+        over_z(ch)
+    spread(Dall, 0, near)
+    u01 += [pass_on(0, k, 2 + index) for index, k in enumerate(far)]
 
     for p in range(1, 4):
         bT[p - 1] = bv[p].T
@@ -130,66 +213,14 @@
                     else:
                         bS[dco * 4 + dx, p, ch] = piece
 
-    def spread(buffer, block):
-        return [
-            send(buffer.at[block, 0, 0], buffer.at[block, 0, k], x_peer[k]) for k in order
-        ]
-
-    def forward(buffer, block, copies):
-        arrive(copies)
-        return [send(buffer.at[block, 0], buffer.at[block, 1], core_peer)]
-
-    def ready_u(block, copies):
-        arrive(copies)
-
-        def body(slot, carry):
-            high, low = split(Uall[block, slot // 4, lax.rem(slot, 4)])
-            lanes = pl.ds(pl.multiple_of(slot * 128, 128), 128)
-            Uh[block, :, lanes] = high
-            Ul[block, :, lanes] = low
-            return carry
-
-        lax.fori_loop(0, 8, body, 0)
-
-    def ready_d(block, copies):
-        arrive(copies)
-
-        def body(slot, carry):
-            high, low = split(Dall[block, slot // 4, lax.rem(slot, 4)])
-            rows = pl.ds(pl.multiple_of(slot * 128, 128), 128)
-            Dh[block, rows, :] = high
-            Dl[block, rows, :] = low
-            return carry
-
-        lax.fori_loop(0, 8, body, 0)
-
-    def share(buffer, me, peers):
-        return [send(buffer.at[me], buffer.at[me], peers[k]) for k in order]
-
-    def total(buffer):
-        return (buffer[0] + buffer[1]) + (buffer[2] + buffer[3])
-
-    x_copies = []
-    for ch in range(NC):
-        arrive(core_copies[ch : ch + 1])
-        P0[co, ch] = P0[co, ch] + Rc[ch]
-        x_copies.append(
-            [send(P0.at[co, ch, ring(x, k)], Rx.at[ch, k - 1], x_peer[k]) for k in order]
-        )
     b_copies = []
     for dco in range(2):
         for dx in range(4):
             if dco or dx:
                 peer = (x_peer[dx] if dco == 0 else core_peer if dx == 0 else xc_peer[dx])
                 b_copies.append(send(bS.at[dco * 4 + dx], bR.at[dco * 4 + dx], peer))
-    u01 = spread(Uall, 0)
-    z_copies = []
-    for ch in range(NC):
-        arrive(x_copies[ch])
-        Z[0, ch, zl] = (P0[co, ch, x] + Rx[ch, 0]) + (Rx[ch, 1] + Rx[ch, 2])
-        z_copies.append(share(Z.at[0, ch], zl, zl_peer))
-    d1 = spread(Dall, 0)
-    ready_u(0, forward(Uall, 0, u01))
+    spread(Dall, 0, far)
+    ready_u(0, u01)
 
     def add_update(p, q, first, count):
         block = BLOCK[(q, p)]
@@ -206,7 +237,8 @@
     stores = []
 
     def output_first(p):
-        OT[p, co, x] = X[p]
+        for a in range(2):
+            OT[p, co, x, a] = X[p, :, a * 128 : (a + 1) * 128]
         out_first[p] = [
             send(OT.at[p, co, x], OT.at[p, co, x], x_peer[k]) for k in order
         ]
@@ -216,10 +248,13 @@
         out_second[p] = [send(OT.at[p, co], OT.at[p, co], core_peer)]
 
     def output_third(p):
-        arrive(out_second[p])
-        copy = pltpu.make_async_copy(OT.at[p], out.at[p], lsem.at[3 + p])
-        copy.start()
-        stores.append(copy)
+        arrive(out_second.get(p, []))
+        for a in range(2):
+            copy = pltpu.make_async_copy(
+                OT.at[p, :, :, a], out.at[p, a], lsem.at[3 + 2 * p + a]
+            )
+            copy.start()
+            stores.append(copy)
 
     pending = {}
     for p in range(1, 4):
@@ -237,37 +272,41 @@
             ])
         output_first(p - 1)
         if p == 1:
-            u02 = spread(Uall, 1)
-            d1 = forward(Dall, 0, d1)
+            spread(Uall, 1, near)
+            d1 = forward(Dall, 0)
         if p == 2:
-            u13 = spread(Uall, 4)
-            u03 = forward(Uall, 3, u03)
-
+            spread(Uall, 3, far)
+            d2 = forward(Dall, 1)
+        if p == 3:
+            d3 = forward(Dall, 2)
+
+        drain()
+        if p == 1:
+            pl.semaphore_wait(beyond, 2)
         h_copies = []
         for ch in range(NC):
             arrive(y_copies[ch])
             own = CT[p - 1, pl.ds(pl.multiple_of(KC * ch + YC * y, 8), YC), :]
             H[p - 1, ch, zh] = (own + Ry[p - 1, ch, 0]) + (Ry[p - 1, ch, 1] + Ry[p - 1, ch, 2])
             h_copies.append(share(H.at[p - 1, ch], zh, zh_peer))
+        output_second(p - 1)
         if p == 1:
+            spread(Uall, 1, far)
+            spread(Uall, 2, near)
             arrive(b_copies)
-            u12 = spread(Uall, 2)
             ready_d(0, d1)
-            ready_u(1, forward(Uall, 1, u02))
-            add_update(2, 0, 0, KS)
-            d2 = spread(Dall, 1)
+            spread(Uall, 2, far)
+            u02 = forward(Uall, 1)
         if p == 2:
-            u23 = spread(Uall, 5)
+            spread(Uall, 4, near)
+            spread(Uall, 4, far)
             ready_d(1, d2)
-            ready_u(3, u03)
-            add_update(3, 0, 0, KS)
-            ready_u(4, forward(Uall, 4, u13))
-            add_update(3, 1, 0, KS)
-            d3 = spread(Dall, 2)
+            spread(Uall, 5, near)
+            u03 = forward(Uall, 3)
         if p == 3:
             ready_d(2, d3)
-        output_second(p - 1)
-
+
+        drain()
         a_copies = []
         for ch in range(NC):
             arrive(h_copies[ch])
@@ -275,10 +314,13 @@
             CY[p - 1, ch, y] = right - total(H.at[p - 1, ch])
             a_copies.append(share(CY.at[p - 1, ch], y, y_peer))
         if p == 1:
-            u12 = forward(Uall, 2, u12)
+            spread(Dall, 1, near)
+            u12 = forward(Uall, 2)
         if p == 2:
-            u23 = forward(Uall, 5, u23)
-
+            spread(Uall, 5, far)
+            u13 = forward(Uall, 4)
+
+        drain()
         z_copies = []
         for ch in range(NC):
             arrive(a_copies[ch])
@@ -286,35 +328,54 @@
             Z[p, ch, zl] = dot3(high, low, Dh[p - 1], Dl[p - 1])
             z_copies.append(share(Z.at[p, ch], zl, zl_peer))
         if p == 1:
-            u03 = spread(Uall, 3)
+            spread(Dall, 1, far)
+            ready_u(1, u02)
+            add_update(2, 0, 0, KS)
+            spread(Uall, 3, near)
             ready_u(2, u12)
-            d2 = forward(Dall, 1, d2)
         if p == 2:
+            spread(Dall, 2, near)
+            u23 = forward(Uall, 5)
+            ready_u(3, u03)
+            add_update(3, 0, 0, KS)
+            ready_u(4, u13)
+            add_update(3, 1, 0, KS)
+            spread(Dall, 2, far)
             ready_u(5, u23)
-            d3 = forward(Dall, 2, d3)
         output_third(p - 1)
-
-    for ch in range(NC):
+        drain()
+
+    last_x, last_core = [], []
+    for ch in range(NC):
+        rows = slice(ch * KC, (ch + 1) * KC)
         arrive(z_copies[ch])
-        X[3, ch * KC : (ch + 1) * KC] = total(Z.at[3, ch])
-    output_first(3)
-    output_second(3)
+        value = total(Z.at[3, ch])
+        for a in range(2):
+            OT[3, co, x, a, rows] = value[:, a * 128 : (a + 1) * 128]
+        piece = OT.at[3, co, x, :, pl.ds(ch * KC, KC)]
+        last_x.append([send(piece, piece, x_peer[k]) for k in order])
+    for ch in range(NC):
+        arrive(last_x[ch])
+        piece = OT.at[3, co, :, :, pl.ds(ch * KC, KC)]
+        last_core.append([send(piece, piece, core_peer)])
+    for ch in range(NC):
+        arrive(last_core[ch])
     output_third(3)
-    for copy in started:
+    for copy in started[marks[-4] :]:
         copy.wait_send()
     for copy in stores:
         copy.wait()
 
 
 def count_sends():
-    return NC + 3 * NC + 7 + 9 * 4 + 4 * 3 * NC + 9 * 3 * NC + 4 * 4
+    return NC + 3 * NC + 7 + 9 * 4 + 3 + 4 * 3 * NC + 9 * 3 * NC + 3 * 4 + 4 * NC
 
 
 def shards(factor, diag_inverse, right_side):
     sends = count_sends()
     solved = pl.pallas_call(
         kernel,
-        out_shape=jax.ShapeDtypeStruct((4, 2, 4, 64, 256), F32),
+        out_shape=jax.ShapeDtypeStruct((4, 2, 2, 4, 64, 128), F32),
         in_specs=[pl.BlockSpec(memory_space=pl.ANY)] * 3,
         out_specs=pl.BlockSpec(memory_space=pl.ANY),
         scratch_shapes=[
@@ -339,10 +400,11 @@
             pltpu.VMEM((3, NC, 4, YC, 1024), F32),
             pltpu.VMEM((3, NC, 4, YC, 1024), F32),
             pltpu.VMEM((4, KS, 256), F32),
-            pltpu.VMEM((4, 2, 4, 64, 256), F32),
-            pltpu.SemaphoreType.DMA((7,)),
+            pltpu.VMEM((4, 2, 4, 2, 64, 128), F32),
+            pltpu.SemaphoreType.DMA((11,)),
             pltpu.SemaphoreType.DMA((sends,)),
             pltpu.SemaphoreType.DMA((sends,)),
+            pltpu.SemaphoreType.REGULAR,
         ],
         compiler_params=pltpu.CompilerParams(
             collective_id=0, has_side_effects=True, vmem_limit_bytes=56 * 1024 * 1024
@@ -353,7 +415,7 @@
         diag_inverse.reshape(1024, 128),
         right_side.reshape(4, 128, 512),
     )
-    pieces = solved.reshape(4, 512, 2, 128).transpose(0, 2, 3, 1)
+    pieces = solved.reshape(8, 512, 128).transpose(0, 2, 1)
     return pieces.reshape(8, 1, 128, 512)
 
 

time: 128 us -> 121 us (0.945)
  Pallas kernels: 124 us -> 117 us
  local copies, waits for them, and re-layouts: 4.62 us -> 2.88 us
    pallas_call x1, Pallas kernels: 124 us -> 117 us  [shards(): pl.pallas_call(kernel, out_shape=jax.ShapeDtypeStruct((4, 2, 2, 4, 64, 12...]
    transpose x1 -> x0, local copies, waits for them, and re-layouts: 2.33 us -> none  [shards(): pieces = solved.reshape(4, 512, 2, 128).transpose(0, 2, 3, 1)]
where the time goes in v2:
time: 121 us; the launch traced here: 120 us
  Pallas kernels  117 us (97%)
  local copies, waits for them, and re-layouts  2.88 us (2%)
    pallas_call x1, Pallas kernels, shards(): pl.pallas_call(kernel, out_shape=jax.ShapeDtypeStruct((4, 2, 2, 4, 64, 12...  117 us
    reshape x1, local copies, waits for them, and re-layouts, shards(): pieces = solved.reshape(8, 512, 128).transpose(0, 2, 1)  2.88 us

profile of v2, /device:TPU:1, one launch (start us, length us, event | category | flops | bytes accessed | tf_op | source)
XLA Modules:
  0.0 120.3 jit_solution(1814308571484501712)
XLA Ops:
  0.0 117.5 %substitution.1 = f32[4,2,2,4,64,128]{5,4,3,2,1,0:T(8,128)} custom-call(f32[4096,128]{1,0:T(8,128)} %bitcast.8, f32[1024,128]{1,0:T(8,128)} %bitcast.10, f32[4,128,512]{2,1,0:T(8,128)} %bitcast.9), custom_call_target="tpu_custom_call" | custom-call | tf_op jit(solution)/shard_map/substitution/pallas_call | solution.py:376
  117.5 2.9 %copy.4 = f32[8,512,128]{1,2,0:T(8,128)} copy(f32[8,512,128]{2,1,0:T(8,128)} %bitcast.7) | data formatting | bytes 4194304 | tf_op jit(solution)/shard_map/reshape | solution.py:418

commit v3 on v2

--- a/solution.py
+++ b/solution.py
@@ -188,10 +188,10 @@
     spread(Uall, 0, near)
     for ch in range(NC):
         over_core(ch)
+    u01 = [send(Uall.at[0, 0, 0], Uall.at[0, 1, 0], core_peer)]
+    for ch in range(NC):
+        over_x(ch)
     spread(Uall, 0, far)
-    u01 = [send(Uall.at[0, 0, 0], Uall.at[0, 1, 0], core_peer)]
-    for ch in range(NC):
-        over_x(ch)
     u01 += [pass_on(0, k, index) for index, k in enumerate(near)]
     for ch in range(NC):
         over_z(ch)
@@ -375,9 +375,9 @@
     sends = count_sends()
     solved = pl.pallas_call(
         kernel,
-        out_shape=jax.ShapeDtypeStruct((4, 2, 2, 4, 64, 128), F32),
+        out_shape=pltpu.VMEM((4, 2, 2, 4, 64, 128), F32),
         in_specs=[pl.BlockSpec(memory_space=pl.ANY)] * 3,
-        out_specs=pl.BlockSpec(memory_space=pl.ANY),
+        out_specs=pl.BlockSpec(memory_space=pltpu.VMEM),
         scratch_shapes=[
             pltpu.VMEM((3072, 128), F32),
             pltpu.VMEM((1024, 128), F32),

time: 121 us -> 119 us (0.983)
  no operation moved by 1% of the time
where the time goes in v3:
time: 119 us
  Pallas kernels  117 us (98%)
  local copies, waits for them, and re-layouts  1.81 us (2%)
    pallas_call x1, Pallas kernels, shards(): pl.pallas_call(kernel, out_shape=pltpu.VMEM((4, 2, 2, 4, 64, 128), F32),...  117 us

profile of v3, /device:TPU:1, one launch (start us, length us, event | category | flops | bytes accessed | tf_op | source)
XLA Modules:
  0.0 119.1 jit_solution(14844528918596410994)
XLA Ops:
  0.0 117.3 %substitution.1 = f32[4,2,2,4,64,128]{5,4,3,2,1,0:T(8,128)S(1)} custom-call(f32[4096,128]{1,0:T(8,128)} %bitcast.8, f32[1024,128]{1,0:T(8,128)} %bitcast.10, f32[4,128,512]{2,1,0:T(8,128)} %bitcast.9), custom_call_target="tpu_custom_call" | custom-call | tf_op jit(solution)/shard_map/substitution/pallas_call | solution.py:376
  117.3 1.8 %copy.4 = f32[8,512,128]{1,2,0:T(8,128)} copy(f32[8,512,128]{2,1,0:T(8,128)S(1)} %bitcast.7) | data formatting | bytes 4194304 | tf_op jit(solution)/shard_map/reshape | solution.py:418

commit v4 on v3

--- a/solution.py
+++ b/solution.py
@@ -130,8 +130,19 @@
             send(buffer.at[block, 0, 0], buffer.at[block, 0, k], x_peer[k]) for k in steps
         )
 
+    def relay(buffer, block):
+        copies = spreads[(buffer is Dall, block)]
+        arrive(copies)
+        half = buffer.shape[3] // 2
+        for k in near:
+            rows = pl.ds(0 if k == 1 else half, half)
+            copies.append(
+                send(buffer.at[block, 0, k, rows], buffer.at[block, 0, 2, rows], x_peer[k])
+            )
+
     def forward(buffer, block):
-        arrive(spreads[(buffer is Dall, block)])
+        copies = spreads[(buffer is Dall, block)]
+        arrive(copies[2:] if len(copies) > 3 else copies)
         return [send(buffer.at[block, 0], buffer.at[block, 1], core_peer)]
 
     def pass_on(block, k, index):
@@ -219,7 +230,6 @@
             if dco or dx:
                 peer = (x_peer[dx] if dco == 0 else core_peer if dx == 0 else xc_peer[dx])
                 b_copies.append(send(bS.at[dco * 4 + dx], bR.at[dco * 4 + dx], peer))
-    spread(Dall, 0, far)
     ready_u(0, u01)
 
     def add_update(p, q, first, count):
@@ -273,7 +283,7 @@
         output_first(p - 1)
         if p == 1:
             spread(Uall, 1, near)
-            d1 = forward(Dall, 0)
+            relay(Dall, 0)
         if p == 2:
             spread(Uall, 3, far)
             d2 = forward(Dall, 1)
@@ -294,7 +304,7 @@
             spread(Uall, 1, far)
             spread(Uall, 2, near)
             arrive(b_copies)
-            ready_d(0, d1)
+            ready_d(0, forward(Dall, 0))
             spread(Uall, 2, far)
             u02 = forward(Uall, 1)
         if p == 2:
@@ -368,7 +378,7 @@
 
 
 def count_sends():
-    return NC + 3 * NC + 7 + 9 * 4 + 3 + 4 * 3 * NC + 9 * 3 * NC + 3 * 4 + 4 * NC
+    return NC + 3 * NC + 7 + 9 * 4 + 1 + 3 + 4 * 3 * NC + 9 * 3 * NC + 3 * 4 + 4 * NC
 
 
 def shards(factor, diag_inverse, right_side):

time: 119 us -> 118 us (level)
    pallas_call x1, Pallas kernels: 117 us -> 116 us  [shards(): pl.pallas_call(kernel, out_shape=pltpu.VMEM((4, 2, 2, 4, 64, 128), F32),...]
where the time goes in v4:
time: 118 us
  Pallas kernels  116 us (98%)
  local copies, waits for them, and re-layouts  1.81 us (2%)
    pallas_call x1, Pallas kernels, shards(): pl.pallas_call(kernel, out_shape=pltpu.VMEM((4, 2, 2, 4, 64, 128), F32),...  116 us

profile of v4, /device:TPU:1, one launch (start us, length us, event | category | flops | bytes accessed | tf_op | source)
XLA Modules:
  0.0 117.5 jit_solution(3333919466159110848)
XLA Ops:
  0.0 115.7 %substitution.1 = f32[4,2,2,4,64,128]{5,4,3,2,1,0:T(8,128)S(1)} custom-call(f32[4096,128]{1,0:T(8,128)} %bitcast.8, f32[1024,128]{1,0:T(8,128)} %bitcast.10, f32[4,128,512]{2,1,0:T(8,128)} %bitcast.9), custom_call_target="tpu_custom_call" | custom-call | tf_op jit(solution)/shard_map/substitution/pallas_call | solution.py:386
  115.7 1.8 %copy.4 = f32[8,512,128]{1,2,0:T(8,128)} copy(f32[8,512,128]{2,1,0:T(8,128)S(1)} %bitcast.7) | data formatting | bytes 4194304 | tf_op jit(solution)/shard_map/reshape | solution.py:428
